TPU v7x, 128 devices: a whole 4x4x4 slice. The times are simulated.
128 devices in a mesh: tm: 16 (over x_hi, y, core), pix: 8 (over x_lo, z).
Axes of the slice: x: 4 (x_hi: 2, x_lo: 2; x = x_hi * 2 + x_lo), y: 4, z: 4, core: 2. Of those that a mesh axis runs over, the one named last changes fastest.
Arguments:
- intensity: bfloat16 [1024, 65536], P('tm', 'pix'), as said below
- labels: int32 [65536], P('pix'), may hold values from 0 to 31, as said below
Outputs:
- correlation: float32 [32, 1024, 1024], P('pix', 'tm')
Inputs may be any that keep to these rules, and one draw needn't show every extreme that they name: `labels`: each aligned run of 128 pixels carries one label; within each device's block of 8192 pixels the runs go in non-decreasing label order, every q-cycle holds between 1 and 4 runs there, and some q-cycle holds exactly 4. `intensity`: every entry is positive.
All inputs are finite; a program needn't handle non-finite values.
Results may differ from a plain program's by a relative error of at most 0.0003.
Values may be sent and summed in bfloat16 or wider, within the bound.
A program may use at most 128 MiB of HBM per device.

v0:
```python
import jax
import jax.numpy as jnp
from jax import lax
from jax.sharding import PartitionSpec as P

CYCLES = 32
CAP = 4


def group_tiles(intensity, labels):
    frames_dev = intensity.shape[0]
    tiles_dev = intensity.shape[1] // 128
    tiles = intensity.reshape(frames_dev, tiles_dev, 128)
    tile_lab = labels.reshape(tiles_dev, 128)[:, 0]
    cycles_all = jnp.arange(CYCLES, dtype=jnp.int32)
    member = tile_lab[None, :] == cycles_all[:, None]
    places = jnp.arange(tiles_dev, dtype=jnp.int32)
    keyed = jnp.where(member, places[None, :], places[None, :] + tiles_dev)
    order = jnp.argsort(keyed, axis=1)[:, :CAP]
    held = jnp.take_along_axis(keyed, order, axis=1) < tiles_dev
    index = jnp.where(held, order, tiles_dev)
    padded = jnp.concatenate([tiles, jnp.zeros((frames_dev, 1, 128), tiles.dtype)], axis=1)
    picked = jnp.take(padded, index.reshape(-1), axis=1)
    grouped = jnp.transpose(picked.reshape(frames_dev, CYCLES, CAP * 128), (1, 0, 2))
    counts = jnp.sum(member.astype(jnp.float32), axis=1) * 128.0
    return (grouped, counts)


def pair_block(left, right):
    return jnp.einsum("rfp,rgp->rfg", left, right, preferred_element_type=jnp.float32)


def per_device(intensity, labels):
    frames_dev = intensity.shape[0]
    grouped, counts = group_tiles(intensity, labels)
    own_totals = jnp.sum(grouped, axis=2, dtype=jnp.float32)
    raw = pair_block(grouped, lax.all_gather(grouped, "tm", axis=1, tiled=True))
    raw, own_totals, counts = (
        lax.psum_scatter(raw, "pix", scatter_dimension=0, tiled=True),
        lax.psum_scatter(own_totals, "pix", scatter_dimension=0, tiled=True),
        lax.psum_scatter(counts, "pix", scatter_dimension=0, tiled=True),
    )
    every_total = lax.all_gather(own_totals, "tm", axis=1, tiled=True)
    own_first = lax.axis_index("tm") * frames_dev
    row_totals = lax.dynamic_slice_in_dim(every_total, own_first, frames_dev, 1)
    return raw * counts[:, None, None] / (row_totals[:, :, None] * every_total[:, None, :])


def solution(mesh):
    placed = (P("tm", "pix"), P("pix"))
    return jax.shard_map(
        per_device, mesh=mesh, in_specs=placed, out_specs=P("pix", "tm", None), check_vma=False
    )
```

profile of v0, /device:TPU:1, one launch (start us, length us, event | category | flops | bytes accessed | tf_op | source)
XLA Modules:
  0.0 332.8 jit_solution(585070707889194805)
XLA Ops:
  6.5 0.0 copy-start
  6.5 0.0 all-gather.3.cloned.1.call-start
  6.5 0.9 slice_reduce_fusion
  7.5 0.1 copy.28
  7.6 1.0 sort.17
  8.6 0.1 copy.29
  8.7 0.1 reshape.78
  8.8 1.3 gather_fusion.1
  10.1 0.1 reshape.81
  10.2 0.1 copy.30
  10.3 0.1 copy.31
  10.4 0.1 broadcast_in_dim.46
  10.6 0.1 copy.33
  10.6 0.1 reshape.69
  10.8 0.0 copy-done
  10.8 0.3 copy_bitcast_fusion
  11.1 0.1 concatenate.3
  11.2 2.2 gather_fusion
  13.3 4.2 %copy.34 = bf16[64,128,128]{2,1,0:T(8,128)(2,1)} copy(bf16[64,128,128]{2,0,1:T(8,128)(2,1)} %bitcast.32) | data formatting | bytes 4194304 | tf_op jit(solution)/shard_map/jit(_take)/gather | solution.py:23
  17.6 3.1 gather.12
  20.7 3.7 %convert_reduce_fusion = (f32[32,64]{1,0:T(8,128)S(1)}, bf16[32,64,512]{2,1,0:T(8,128)(2,1)}) fusion(bf16[64,32,512]{2,1,0:T(8,128)(2,1)S(1)} %gather.12, pred[32,512]{1,0:T(8,128)(4,1)S(1)} %bitcast.34), kind=kLoop, calls=%fused_computation.2 | loop fusion | flops 3143680 | bytes 4218880 | tf_op jit(solution)/shard_map/reduce_sum | solution.py:36
  24.4 0.0 copy-start.1
  24.4 0.0 all-gather.3.cloned.1.call-update
  24.4 0.0 reduce-scatter.2.cloned.1.call-start
  24.5 189.6 %all-gather.3.cloned.1.call-done = bf16[32,1024,512]{2,1,0:T(8,128)(2,1)} async-done(((bf16[32,64,512]{2,1,0:T(8,128)(2,1)}), bf16[32,1024,512]{2,1,0:T(8,128)(2,1)}) %all-gather.3.cloned.1.call-update) | async-done | bytes 33554448 | tf_op jit(solution)/shard_map/all_gather | solution.py:37
  214.1 0.0 copy-done.1
  214.1 18.3 %fusion.5 = f32[32,64,1024]{2,1,0:T(8,128)} fusion(bf16[32,64,512]{2,1,0:T(8,128)(2,1)S(1)} %copy-done.1, bf16[32,1024,512]{2,1,0:T(8,128)(2,1)} %all-gather.3.cloned.1.call-done), kind=kOutput, calls=%fused_computation.25 | convolution fusion | flops 2147483648 | bytes 44040192 | tf_op jit(solution)/shard_map/rfp,rgp->rfg/dot_general | solution.py:30
  232.4 0.0 copy-start.2
  232.4 0.0 reduce-scatter.2.cloned.1.call-update
  232.5 0.6 copy-done.2
  233.1 0.6 dynamic-slice.1
  234.3 0.1 convert_reduce_fusion.1
  234.5 30.1 %all-reduce.3 = (f32[32,64]{1,0:T(8,128)S(1)}, f32[32]{0:T(128)S(1)}) all-reduce(f32[32,64]{1,0:T(8,128)S(1)} %get-tuple-element.9, f32[32]{0:T(128)S(1)} %broadcast_multiply_fusion), channel_id=4, replica_groups=mesh['tm'=16,'pix'=8] {'pix'}, use_global_device_ids=true, to_apply=%region_5.6.clone | all-reduce | flops 2080 | bytes 16640
  264.6 0.1 dynamic-slice.2
  264.7 26.7 %all-gather = f32[16,64,4]{1,2,0:T(4,128)S(1)} all-gather(f32[1,64,4]{1,2,0:T(4,128)S(1)} %dynamic-slice_bitcast_fusion), channel_id=1, replica_groups=mesh['tm'=16,'pix'=8] {'tm'}, dimensions={0}, use_global_device_ids=true | all-gather | bytes 17408 | tf_op jit(solution)/shard_map/all_gather | solution.py:43
  291.4 0.1 reshape.90
  291.5 0.1 dynamic-slice_bitcast_fusion.1
  291.5 31.9 %reduce-scatter.2.cloned.1.call-done = f32[4,64,1024]{2,1,0:T(8,128)} async-done(((f32[32,64,1024]{2,1,0:T(8,128)}), f32[4,64,1024]{2,1,0:T(8,128)}) %reduce-scatter.2.cloned.1.call-update) | async-done | bytes 1048592 | tf_op jit(solution)/shard_map/reduce_scatter | solution.py:39
  323.4 2.6 multiply_divide_fusion
  (11 shorter events, 0.1 us)
Async XLA Ops:
  6.5 4.2 %copy-start = (bf16[64,8192]{1,0:T(8,128)(2,1)S(1)}, bf16[64,8192]{1,0:T(8,128)(2,1)}, u32[]{:S(2)}) copy-start(bf16[64,8192]{1,0:T(8,128)(2,1)} %param.2) | copy-start | bytes 3145732
  6.5 207.6 %all-gather.3.cloned.1.call-start = ((), (), s32[]{:S(2)}) async-start(), calls=%async_computation.1 | async-start | bytes 35651584 | tf_op jit(solution)/shard_map/all_gather | solution.py:37
  24.4 189.7 %copy-start.1 = (bf16[32,64,512]{2,1,0:T(8,128)(2,1)S(1)}, bf16[32,64,512]{2,1,0:T(8,128)(2,1)}, u32[]{:S(2)}) copy-start(bf16[32,64,512]{2,1,0:T(8,128)(2,1)} %get-tuple-element.10) | copy-start | bytes 6291460
  24.4 299.0 %reduce-scatter.2.cloned.1.call-start = ((), (), s32[]{:S(2)}) async-start(), calls=%async_computation.2 | async-start | bytes 9437184 | tf_op jit(solution)/shard_map/reduce_scatter | solution.py:39
  232.4 0.7 copy-start.2
Sparse Core Ops, SparseCore 0:
  24.6 189.5 all-gather.2
  232.6 90.7 reduce-scatter.1
where the time goes:
time: 333 us
  waiting for transfers between devices  222 us (67%)
  blocking collectives  56.8 us (17%)
  matrix products  18.3 us (5%)
  local copies, waits for them, and re-layouts  14.4 us (4%)
  between operations  14.2 us (4%)
  other arithmetic  7.49 us (2%)
    all_gather x1, waiting for transfers between devices, per_device(): raw = pair_block(grouped, lax.all_gather(grouped, 'tm', axis=1, tiled=True))  190 us
    reduce_scatter x1, waiting for transfers between devices, per_device(): lax.psum_scatter(raw, 'pix', scatter_dimension=0, tiled=True)  31.9 us
    unnamed x1, blocking collectives  30.1 us
    all_gather x1, blocking collectives, per_device(): every_total = lax.all_gather(own_totals, 'tm', axis=1, tiled=True)  26.7 us
    dot_general x1, matrix products, pair_block(): jnp.einsum('rfp,rgp->rfg', left, right, preferred_element_type=jnp.float32)  18.3 us
    gather x3, local copies, waits for them, and re-layouts, group_tiles(): picked = jnp.take(padded, index.reshape(-1), axis=1)  9.5 us
  transfers between devices with their start and end apart: 2, of which 2 were waited for; matrix products, arithmetic and copies ran while one was open for 0% of the time, Pallas kernels for 0%

commit v1 on v0

v1 whole, which is shorter than its diff:
```python
import jax
import jax.numpy as jnp
from jax import lax
from jax.experimental import pallas as pl
from jax.experimental.pallas import tpu as pltpu
from jax.sharding import PartitionSpec as P

CYCLES = 32
CAP = 4
MESH = pl.DeviceIdType.MESH
F32 = jnp.float32
BF16 = jnp.bfloat16
ROWS_A = 64
ROWS_B = 128
ROWS_C = 104


def nt(left, right):
    return lax.dot_general(left, right, (((1,), (1,)), ((), ())), preferred_element_type=F32)


def kernel(
    places, masks, counts, x_ref, out_ref,
    obuf, y1buf, fbuf, y2buf,
    ga, gb, gc, ra1, ra2, ra3, rb1, rb2, rb3, rc1, rc2, rc3,
    s12, s3, s4, s5, s6, r12, r3, r4, r5, r6, kept1, kept2,
    gs, gr, as_, ar, bs, br, cs, cr, fs, fr,
):
    tm, pix = lax.axis_index("tm"), lax.axis_index("pix")
    core = tm % 2
    y = (tm // 2) % 4
    kx = tm // 8
    ky = y // 2
    z = pix % 4
    xl = pix // 4
    sib = 1 - core

    def at(k, yy, c):
        return ((k * 4 + yy % 4) * 2 + c, pix)

    def flip(a, b):
        return (a + b) % 2

    z1 = z + 1 - 2 * (z % 2)
    z3 = 3 - z
    z2 = (z + 2) % 4
    dev_sib = at(kx, y, sib)
    dev_z1 = (tm, xl * 4 + z1)
    dev_z3 = (tm, xl * 4 + z3)
    dev_x = (tm, (1 - xl) * 4 + z)

    barrier = pltpu.get_barrier_semaphore()
    friends = [dev_sib, dev_z1, dev_z3, dev_x]
    for c in range(2):
        friends += [at(kx, y + 1, c), at(kx, y + 3, c), at(kx, y + 2, c), at(1 - kx, y, c)]
    for d in friends:
        pl.semaphore_signal(barrier, inc=1, device_id=d, device_id_type=MESH)
    mine = pl.ds(core * 64, 64)
    for t in range(x_ref.shape[1] // 128):
        obuf[t, mine] = x_ref[:, t * 128 : t * 128 + 128]
    pl.semaphore_wait(barrier, len(friends))

    def send(src, dst, ss, rs, k, d):
        r = pltpu.make_async_remote_copy(
            src_ref=src, dst_ref=dst, send_sem=ss.at[k], recv_sem=rs.at[k],
            device_id=d, device_id_type=MESH,
        )
        r.start()
        return r

    every = pl.ds(0, obuf.shape[0])
    src = obuf.at[every, mine]
    cp_sib = send(src, obuf.at[every, mine], gs, gr, 0, dev_sib)
    cp_f = send(src, fbuf.at[every, mine], gs, gr, 1, at(1 - kx, y, core))
    cp_y1 = send(src, y1buf.at[every, mine], gs, gr, 2, at(kx, y + 3, core))
    cp_y2 = send(src, y2buf, gs, gr, 3, at(kx, y + 2, flip(core, 1 - ky)))

    fk = pl.ds(flip(core, kx) * 64, 64)

    def span(r):
        tile = places[r]
        mask = jnp.broadcast_to(masks[pl.ds(r, 1), :], (8, CAP * 128)).astype(BF16)
        return tile, mask, counts[pl.ds(r, 1), :]

    def window(ref, tile, rows):
        return jnp.concatenate([ref[tile + k, rows] for k in range(CAP)], axis=1)

    def slot(r):
        return r // 16, (r // 4) % 4, r % 4

    def compute_a():
        @pl.loop(0, CYCLES)
        def _(r):
            tile, mask, _ = span(r)
            right = window(obuf, tile, slice(None)) * mask[0:1]
            ga[slot(r)] = nt(window(obuf, tile, mine), right)

    def compute_b():
        @pl.loop(0, CYCLES)
        def _(r):
            tile, mask, _ = span(r)
            right = jnp.concatenate([window(obuf, tile, mine), window(fbuf, tile, mine)], axis=0) * mask[0:1]
            gb[slot(r)] = nt(window(y1buf, tile, slice(None)), right)

    def compute_c():
        @pl.loop(0, CYCLES)
        def _(r):
            tile, mask, count = span(r)
            right = jnp.concatenate([window(obuf, tile, mine), window(fbuf, tile, mine)], axis=0)
            far = jnp.concatenate([window(y2buf, tile, slice(None)), window(fbuf, tile, fk)], axis=0)
            masked = right * mask[0:1]
            both = nt(far, masked)
            i, k, j = slot(r)
            gc[i, k, j, 0:64] = both[0:64]
            gc[i, k, j, 64:96] = jnp.concatenate([both[64:96, 0:64], both[96:128, 0:64]], axis=1)
            t0 = nt(mask, window(obuf, tile, slice(None)))
            t1 = nt(mask, window(y1buf, tile, slice(None)))
            t2 = nt(mask, right)
            t3 = nt(mask, far)
            row = lax.broadcasted_iota(jnp.int32, (8, 128), 0)
            stats = jnp.where(row == 0, t0, jnp.where(row == 1, t1, jnp.where(row == 2, t2, t3)))
            gc[i, k, j, 96:104] = jnp.where(row < 4, stats, count)

    lo, hi = pl.ds(0, 2), pl.ds(2, 2)
    both_x = pl.ds(0, 2)

    class Sum:
        def __init__(self, g, r1, r2, r3, ss, rs):
            self.g, self.r1, self.r2, self.r3, self.ss, self.rs = g, r1, r2, r3, ss, rs

        def first(self):
            g, r1 = self.g, self.r1
            self.c1 = [
                send(g.at[both_x, z2, lo], r1.at[0, 0], self.ss, self.rs, 0, dev_z1),
                send(g.at[both_x, z2, hi], r1.at[1, 0], self.ss, self.rs, 1, dev_z3),
                send(g.at[both_x, z1, lo], r1.at[0, 1], self.ss, self.rs, 2, dev_z1),
                send(g.at[both_x, z3, hi], r1.at[1, 1], self.ss, self.rs, 3, dev_z3),
            ]

        def second(self):
            g, r1, r2 = self.g, self.r1, self.r2
            self.c2 = []
            for p, (js, zz, d) in enumerate(((0, z3, dev_z3), (2, z1, dev_z1))):
                self.c1[p].wait()
                for i in range(2):
                    for j in range(2):
                        g[i, zz, js + j] += r1[p, 0, i, j]
                self.c2.append(send(g.at[both_x, zz, pl.ds(js, 2)], r2.at[p], self.ss, self.rs, 4 + p, d))
            for p in range(2):
                self.c1[2 + p].wait()
                for i in range(2):
                    for j in range(2):
                        g[i, z, 2 * p + j] += r1[p, 1, i, j]

        def third(self):
            g, r2 = self.g, self.r2
            for p in range(2):
                self.c2[p].wait()
                for j in range(2):
                    g[1 - xl, z, 2 * p + j] += r2[p, 1 - xl, j]
            self.c3 = send(g.at[1 - xl, z], self.r3, self.ss, self.rs, 6, dev_x)
            for p in range(2):
                for j in range(2):
                    g[xl, z, 2 * p + j] += r2[p, xl, j]

        def last(self):
            self.c3.wait()

        def total(self, j):
            return self.g[xl, z, j] + self.r3[j]

    sum_a = Sum(ga, ra1, ra2, ra3, as_, ar)
    sum_b = Sum(gb, rb1, rb2, rb3, bs, br)
    sum_c = Sum(gc, rc1, rc2, rc3, cs, cr)

    cp_sib.wait()
    compute_a()
    sum_a.first()
    cp_f.wait()
    fw_f = send(fbuf.at[every, mine], fbuf.at[every, mine], gs, gr, 4, dev_sib)
    cp_y1.wait()
    fw_y1 = send(y1buf.at[every, mine], y1buf.at[every, mine], gs, gr, 5, dev_sib)
    sum_a.second()
    fw_f.wait()
    fw_y1.wait()
    compute_b()
    sum_b.first()
    sum_a.third()
    cp_y2.wait()
    compute_c()
    sum_c.first()
    sum_b.second()
    sum_c.second()
    sum_b.third()
    sum_c.third()
    sum_a.last()
    sum_b.last()
    sum_c.last()

    here = kx * 4 + y
    near = kx * 4 + (y + 1) % 4
    prev = kx * 4 + (y + 3) % 4
    opp = kx * 4 + (y + 2) % 4
    cross = (1 - kx) * 4 + y
    cross_near = (1 - kx) * 4 + (y + 1) % 4
    cross_prev = (1 - kx) * 4 + (y + 3) % 4
    cross_opp = (1 - kx) * 4 + (y + 2) % 4
    k2 = flip(core, ky)
    k1 = flip(core, kx)

    def place(j, chip, value):
        out_ref[j, :, pl.ds(pl.multiple_of(chip * 128, 128), 128)] = value

    def ordered(k, local, remote):
        first = jnp.where(k == 0, local, remote)
        second = jnp.where(k == 0, remote, local)
        return jnp.concatenate([first, second], axis=1)

    for j in range(4):
        c_all = sum_c.total(j)
        stats = c_all[96:104]
        cols = stats.T
        count = stats[4:5]
        t_all, t_right = stats[0:1], stats[2:3]
        place(j, here, sum_a.total(j) * count / (cols[0:64, 2:3] * t_all))
        b = sum_b.total(j) * count / (cols[:, 1:2] * t_right)
        s12[0, j] = b[0:64]
        s12[1, j] = b[64:128]
        bt = b.T
        place(j, near, bt[0:64])
        s4[j] = bt[64:128]
        c2 = c_all[0:64] * count / (cols[0:64, 3:4] * t_right)
        s3[j] = c2
        c2t = c2.T
        kept2[j] = c2t[0:64]
        s5[j] = jnp.concatenate([c2t[64:96], c2t[96:128]], axis=1)
        f = jnp.concatenate([c_all[64:96, 0:64], c_all[64:96, 64:128]], axis=0)
        f = f * count[:, 0:64] / (cols[64:128, 3:4] * t_right[:, 0:64])
        s6[j] = jnp.concatenate([f[0:32], f[32:64]], axis=1)
        kept1[j] = f.T

    def copy12(k, landing):
        return pltpu.make_async_remote_copy(
            src_ref=s12.at[k], dst_ref=r12.at[landing], send_sem=fs.at[k], recv_sem=fr.at[landing],
            device_id=at(kx, y + 1, k), device_id_type=MESH,
        )

    for k in range(2):
        copy12(k, core).start()
    m = [
        send(s3, r3, fs, fr, 2, at(kx, y + 2, k2)),
        send(s4, r4, fs, fr, 3, at(1 - kx, y, core)),
        send(s5, r5, fs, fr, 4, at(1 - kx, y, core)),
        send(s6, r6, fs, fr, 5, at(1 - kx, y, k1)),
    ]
    for k in range(2):
        copy12(k, core).wait_send()
        copy12(k, k).wait_recv()
    for c in m:
        c.wait()

    for j in range(4):
        p, q = r12[0, j], r12[1, j]
        place(j, prev, jnp.concatenate([p[:, 0:64], q[:, 0:64]], axis=1))
        place(j, cross_prev, jnp.concatenate([p[:, 64:128], q[:, 64:128]], axis=1))
        place(j, cross_near, r4[j])
        far = r3[j]
        place(j, opp, ordered(k2, kept2[j], far[:, 0:64]))
        five = r5[j]
        five = jnp.concatenate([five[:, 0:64], five[:, 64:128]], axis=0)
        place(j, cross_opp, ordered(k2, five, far[:, 64:128]))
        six = r6[j]
        six = jnp.concatenate([six[:, 0:64], six[:, 64:128]], axis=0)
        place(j, cross, ordered(k1, kept1[j], six))


def per_device(intensity, labels):
    tile_lab = labels.reshape(-1, 128)[:, 0]
    cycles = jnp.arange(CYCLES, dtype=jnp.int32)
    first = jnp.sum((tile_lab[None, :] < cycles[:, None]).astype(jnp.int32), axis=1)
    count = jnp.sum((tile_lab[None, :] == cycles[:, None]).astype(jnp.int32), axis=1)
    places = jnp.minimum(first, tile_lab.shape[0] - CAP)
    low = (first - places) * 128
    high = low + count * 128
    lane = jnp.arange(CAP * 128, dtype=jnp.int32)[None, :]
    masks = ((lane >= low[:, None]) & (lane < high[:, None])).astype(F32)
    counts = jnp.broadcast_to((count * 128).astype(F32)[:, None], (CYCLES, 128))
    pix_dev = intensity.shape[1]
    dma = pltpu.SemaphoreType.DMA

    def sums(rows):
        return [
            pltpu.VMEM((2, 2, 2, 2, rows, 128), F32),
            pltpu.VMEM((2, 2, 2, rows, 128), F32),
            pltpu.VMEM((4, rows, 128), F32),
        ]

    messages = [
        pltpu.VMEM((2, 4, 64, 128), F32),
        pltpu.VMEM((4, 64, 128), F32),
        pltpu.VMEM((4, 64, 128), F32),
        pltpu.VMEM((4, 32, 128), F32),
        pltpu.VMEM((4, 32, 128), F32),
    ]
    return pl.pallas_call(
        kernel,
        out_shape=jax.ShapeDtypeStruct((4, 64, 1024), F32),
        in_specs=[
            pl.BlockSpec(memory_space=pltpu.SMEM),
            pl.BlockSpec(memory_space=pltpu.VMEM),
            pl.BlockSpec(memory_space=pltpu.VMEM),
            pl.BlockSpec(memory_space=pltpu.VMEM),
        ],
        out_specs=pl.BlockSpec(memory_space=pltpu.VMEM),
        scratch_shapes=[
            pltpu.VMEM((pix_dev // 128, 128, 128), BF16),
            pltpu.VMEM((pix_dev // 128, 128, 128), BF16),
            pltpu.VMEM((pix_dev // 128, 128, 128), BF16),
            pltpu.VMEM((pix_dev // 128, 64, 128), BF16),
            pltpu.VMEM((2, 4, 4, ROWS_A, 128), F32),
            pltpu.VMEM((2, 4, 4, ROWS_B, 128), F32),
            pltpu.VMEM((2, 4, 4, ROWS_C, 128), F32),
            *sums(ROWS_A), *sums(ROWS_B), *sums(ROWS_C),
            *messages, *messages,
            pltpu.VMEM((4, 64, 64), F32),
            pltpu.VMEM((4, 64, 64), F32),
            dma((6,)), dma((6,)), dma((7,)), dma((7,)), dma((7,)), dma((7,)),
            dma((7,)), dma((7,)), dma((6,)), dma((6,)),
        ],
        compiler_params=pltpu.CompilerParams(
            collective_id=0, has_side_effects=True, vmem_limit_bytes=48 * 2**20
        ),
    )(places, masks, counts, intensity)


def solution(mesh):
    placed = (P("tm", "pix"), P("pix"))
    return jax.shard_map(
        per_device, mesh=mesh, in_specs=placed, out_specs=P("pix", "tm", None), check_vma=False
    )
```

time: 333 us -> 107 us (0.32)
  waiting for transfers between devices: 222 us -> 0 us
  Pallas kernels: 0 us -> 104 us
  blocking collectives: 56.8 us -> 0 us
  matrix products: 18.3 us -> 0 us
  between operations: 14.2 us -> 0.04 us
  local copies, waits for them, and re-layouts: 14.4 us -> 3.12 us
  other arithmetic: 7.49 us -> 0.2 us
    all_gather x1 -> x0, waiting for transfers between devices: 190 us -> none  [per_device(): raw = pair_block(grouped, lax.all_gather(grouped, 'tm', axis=1, tiled=True))]
    pallas_call x0 -> x1, Pallas kernels: none -> 104 us  [per_device(): pl.pallas_call(kernel, out_shape=jax.ShapeDtypeStruct((4, 64, 1024), F32)...]
    reduce_scatter x1 -> x0, waiting for transfers between devices: 31.9 us -> none  [per_device(): lax.psum_scatter(raw, 'pix', scatter_dimension=0, tiled=True)]
    unnamed x1 -> x0, blocking collectives: 30.1 us -> none
    all_gather x1 -> x0, blocking collectives: 26.7 us -> none  [per_device(): every_total = lax.all_gather(own_totals, 'tm', axis=1, tiled=True)]
    dot_general x1 -> x0, matrix products: 18.3 us -> none  [pair_block(): jnp.einsum('rfp,rgp->rfg', left, right, preferred_element_type=jnp.float32)]
    gather x8 -> x0, local copies, waits for them, and re-layouts: 11.1 us -> none  [the longest x3 9.5 us: group_tiles(): picked = jnp.take(padded, index.reshape(-1), axis=1)]
    reduce_sum x2 -> x1, other arithmetic: 3.85 us -> 0.12 us  [per_device(): jnp.sum((tile_lab[None, :] == cycles[:, None]).astype(jnp.int32), axis=1)]
  transfers between devices with their start and end apart: 2 -> 0, of which waited for: 2 -> 0; matrix products, arithmetic and copies ran while one was open for 0% -> 0% of each run, Pallas kernels for 0% -> 0%
where the time goes in v1:
time: 107 us
  Pallas kernels  104 us (97%)
  local copies, waits for them, and re-layouts  3.12 us (3%)
    pallas_call x1, Pallas kernels, per_device(): pl.pallas_call(kernel, out_shape=jax.ShapeDtypeStruct((4, 64, 1024), F32)...  104 us
    unnamed x3, local copies, waits for them, and re-layouts  2.19 us

profile of v1, /device:TPU:1, one launch (start us, length us, event | category | flops | bytes accessed | tf_op | source)
XLA Modules:
  0.0 106.9 jit_solution(11011085105685523682)
XLA Ops:
  0.0 0.9 slice_reduce_fusion
  0.9 0.1 convert_reduce_fusion
  1.0 0.1 broadcast_in_dim.2.counts
  1.1 0.1 fusion.1.masks
  1.2 0.0 copy-start
  1.2 1.2 %copy-done = bf16[64,8192]{1,0:T(8,128)(2,1)S(1)} copy-done((bf16[64,8192]{1,0:T(8,128)(2,1)S(1)}, bf16[64,8192]{1,0:T(8,128)(2,1)}, u32[]{:S(2)}) %copy-start) | copy-done | bytes 1048600
  2.4 103.5 %shard_map.28 = f32[4,64,1024]{2,1,0:T(8,128)S(1)} custom-call(s32[32]{0:T(128)S(1)} %get-tuple-element.10.places, f32[32,512]{1,0:T(8,128)S(1)} %fusion.1.masks, f32[32,128]{1,0:T(8,128)S(1)} %broadcast_in_dim.2.counts, bf16[64,8192]{1,0:T(8,128)(2,1)S(1)} %copy-done), custom_call_target="tpu_custom_call" | custom-call | tf_op jit(solution)/shard_map/pallas_call | solution.py:305
  105.9 1.0 copy.4
  (1 shorter events, 0.0 us)
Async XLA Ops:
  1.2 1.2 %copy-start = (bf16[64,8192]{1,0:T(8,128)(2,1)S(1)}, bf16[64,8192]{1,0:T(8,128)(2,1)}, u32[]{:S(2)}) copy-start(bf16[64,8192]{1,0:T(8,128)(2,1)} %x_ref.1) | copy-start | bytes 3145732

commit v2 on v0

v2 whole, which is shorter than its diff:
```python
import jax
import jax.numpy as jnp
from jax import lax
from jax.experimental import pallas as pl
from jax.experimental.pallas import tpu as pltpu
from jax.sharding import PartitionSpec as P

CYCLES = 32
CAP = 4
MESH = pl.DeviceIdType.MESH
F32 = jnp.float32
BF16 = jnp.bfloat16
FRAMES_DEV = 64
TOP = 32768.0
STEPS = 2048.0
CODE = jnp.int16
SUMS = (64, 64, 96, 64)
RELAYED = 44


def nt(left, right):
    return lax.dot_general(left, right, (((1,), (1,)), ((), ())), preferred_element_type=F32)


def encode(value):
    level = jnp.log2(jnp.maximum(value, 1.0 / 65536.0)) * STEPS
    return jnp.round(level).astype(jnp.int32).astype(CODE)


def decode(code):
    return jnp.exp2(code.astype(jnp.int32).astype(F32) * (1.0 / STEPS))


def fold(block):
    return jnp.concatenate([block[0:32], block[32:64]], axis=1)


def unfold(block):
    return jnp.concatenate([block[:, 0:64], block[:, 64:128]], axis=0)


def kernel(places, masks, counts, x_ref, out_ref, *refs):
    refs = list(refs)

    def take(n):
        got = refs[:n]
        del refs[:n]
        return got

    xv, ownb, obuf, fbuf, y1buf, y2buf, relay = take(7)
    part, landed, tt, tr = take(4)
    col_y1, col_y2, col_f = take(3)
    row_o, row_f, row_2 = take(3)
    sets = [take(9) for _ in SUMS]
    s1, s2, s3, s4, s5, s6, s7 = take(7)
    r1, r2, r3, r4, r5, r6, r7 = take(7)
    kept0, kept1, kept2 = take(3)
    own_sem, gs, gr, ps, pr, ts, tsr, fs, fr = take(9)

    tm, pix = lax.axis_index("tm"), lax.axis_index("pix")
    core = tm % 2
    y = (tm // 2) % 4
    kx = tm // 8
    ky = y // 2
    z = pix % 4
    xl = pix // 4
    sib = 1 - core

    def at(k, yy, c):
        return ((k * 4 + yy % 4) * 2 + c, pix)

    def flip(a, b):
        return (a + b) % 2

    k2 = flip(core, ky)
    k1 = flip(core, kx)
    z1 = z + 1 - 2 * (z % 2)
    z3 = 3 - z
    z2 = (z + 2) % 4
    dev_sib = at(kx, y, sib)
    dev_z1 = (tm, xl * 4 + z1)
    dev_z3 = (tm, xl * 4 + z3)
    dev_x = (tm, (1 - xl) * 4 + z)
    near_core = at(kx, y + 1, core)

    own = pltpu.make_async_copy(x_ref, xv, own_sem)
    own.start()
    barrier = pltpu.get_barrier_semaphore()
    friends = [dev_sib] + [(tm, (pix + q) % 8) for q in range(1, 8)]
    for c in range(2):
        friends += [at(kx, y + 1, c), at(kx, y + 3, c), at(kx, y + 2, c), at(1 - kx, y, c)]
    for d in friends:
        pl.semaphore_signal(barrier, inc=1, device_id=d, device_id_type=MESH)
    mine = pl.ds(core * 64, 64)
    own.wait()
    for t in range(x_ref.shape[1] // 128):
        block = xv[:, t * 128 : t * 128 + 128]
        ownb[t] = block
        obuf[t, mine] = block
    pl.semaphore_wait(barrier, len(friends))

    def copy(src, dst, ss, rs, d):
        return pltpu.make_async_remote_copy(
            src_ref=src, dst_ref=dst, send_sem=ss, recv_sem=rs, device_id=d, device_id_type=MESH
        )

    def send(src, dst, ss, rs, k, d):
        r = copy(src, dst, ss.at[k], rs.at[k], d)
        r.start()
        return r

    every = pl.ds(0, obuf.shape[0])
    pre = pl.ds(0, RELAYED)
    post = pl.ds(RELAYED, obuf.shape[0] - RELAYED)
    dev_prev = at(kx, y + 3, core)
    cp_y1p = send(ownb.at[post], y1buf.at[post], gs, gr, 1, dev_prev)
    cp_rel = send(ownb.at[pre], relay, gs, gr, 2, near_core)
    cp_y1q = send(ownb.at[pre], y1buf.at[pre], gs, gr, 5, dev_prev)
    cp_sib = send(ownb, obuf.at[every, mine], gs, gr, 0, dev_sib)

    def span(r):
        tile = places[r]
        mask = jnp.broadcast_to(masks[pl.ds(r, 1), :], (8, CAP * 128)).astype(BF16)
        return tile, mask

    def window(ref, tile, rows):
        return jnp.concatenate([ref[tile + k, rows] for k in range(CAP)], axis=1)

    def slot(r):
        return r // 16, (r // 4) % 4, r % 4

    def cycles(body):
        @pl.loop(0, CYCLES, unroll=4)
        def _(r):
            body(r)

    ga, gb, gd, gc = [q[0] for q in sets]
    whole = slice(None)

    def scaled(r, g, col, rows):
        return g * col * rows[pl.ds(r, 1), :]

    def totals_own(r):
        tile, mask = span(r)
        t = nt(mask, window(ownb, tile, whole))
        part[pl.ds(r, 1)] = jnp.concatenate([t[0:1], counts[pl.ds(r, 1), 0:64]], axis=1)

    def gram_a(r):
        tile, mask = span(r)
        right = window(obuf, tile, whole) * mask[0:1]
        ga[slot(r)] = nt(window(obuf, tile, mine), right)

    def gram_b(r):
        tile, mask = span(r)
        right = window(obuf, tile, whole) * mask[0:1]
        gb[slot(r)] = scaled(r, nt(window(y1buf, tile, whole), right), col_y1[r], row_o)

    def two(tile, mask):
        right = jnp.concatenate([window(obuf, tile, mine), window(fbuf, tile, mine)], axis=0)
        return right * mask[0:1]

    def gram_d(r):
        tile, mask = span(r)
        i, k, j = slot(r)
        right = window(fbuf, tile, whole) * mask[0:1]
        gd[i, k, j, 0:64] = scaled(r, nt(window(y1buf, tile, whole), right), col_y1[r], row_f)
        fk = pl.ds(k1 * 64, 64)
        right = window(obuf, tile, mine) * mask[0:1]
        g = nt(window(fbuf, tile, fk), right)
        g = g * col_f[r, :, 0:64] * row_2[pl.ds(r, 1), 0:64]
        gd[i, k, j, 64:96] = fold(g)

    def gram_c(r):
        tile, mask = span(r)
        g = nt(window(y2buf, tile, whole), two(tile, mask))
        gc[slot(r)] = scaled(r, g, col_y2[r], row_2)

    lo, hi = pl.ds(0, 2), pl.ds(2, 2)
    both_x = pl.ds(0, 2)

    class Sum:
        def __init__(self, coded, g, e1, e2, e3, r1, r2, r3, ss, rs):
            self.encode = encode if coded else (lambda v: v)
            self.decode = decode if coded else (lambda v: v)
            self.g, self.e, self.r = g, (e1, e2, e3), (r1, r2, r3)
            self.ss, self.rs = ss, rs

        def first(self):
            g, e1, r1 = self.g, self.e[0], self.r[0]
            self.c1 = []
            for w, (za, zb) in enumerate(((z2, z2), (z1, z3))):
                for p, (js, zz, d) in enumerate(((0, za, dev_z1), (2, zb, dev_z3))):
                    for i in range(2):
                        for j in range(2):
                            e1[p, w, i, j] = self.encode(g[i, zz, js + j])
                    self.c1.append(send(e1.at[p, w], r1.at[p, w], self.ss, self.rs, 2 * w + p, d))

        def second(self):
            g, e2, r1, r2 = self.g, self.e[1], self.r[0], self.r[1]
            self.c2 = []
            for p, (js, zz, d) in enumerate(((0, z3, dev_z3), (2, z1, dev_z1))):
                self.c1[p].wait()
                for i in range(2):
                    for j in range(2):
                        e2[p, i, j] = self.encode(g[i, zz, js + j] + self.decode(r1[p, 0, i, j]))
                self.c2.append(send(e2.at[p], r2.at[p], self.ss, self.rs, 4 + p, d))
            for p in range(2):
                self.c1[2 + p].wait()
                for i in range(2):
                    for j in range(2):
                        g[i, z, 2 * p + j] += self.decode(r1[p, 1, i, j])

        def third(self):
            g, e3, r2 = self.g, self.e[2], self.r[1]
            for p in range(2):
                self.c2[p].wait()
                for j in range(2):
                    e3[2 * p + j] = self.encode(g[1 - xl, z, 2 * p + j] + self.decode(r2[p, 1 - xl, j]))
            self.c3 = send(e3, self.r[2], self.ss, self.rs, 6, dev_x)
            for p in range(2):
                for j in range(2):
                    g[xl, z, 2 * p + j] += self.decode(r2[p, xl, j])

        def last(self):
            self.c3.wait()

        def total(self, j):
            return self.g[xl, z, j] + self.decode(self.r[2][j])

    sum_a, sum_b, sum_d, sum_c = [Sum(n > 0, *q) for n, q in enumerate(sets)]

    cycles(totals_own)
    cp = []
    for q in range(1, 8):
        cp.append(send(part, landed.at[q - 1], ps, pr, q - 1, (tm, (pix + q) % 8)))
    cp_f = send(ownb, fbuf.at[every, mine], gs, gr, 3, at(1 - kx, y, core))
    cp_sib.wait()
    cycles(gram_a)
    sum_a.first()
    cp_y1p.wait()
    cp_fp = send(y1buf.at[post], y2buf.at[post], gs, gr, 6, at(kx, y + 3, flip(core, ((y + 3) % 4) // 2)))
    total = part[...]
    for q in range(7):
        cp[q].wait()
        total = total + landed[q]
    tt[...] = total
    tcopies = [
        send(tt, tr.at[0], ts, tsr, 0, dev_sib),
        send(tt, tr.at[1], ts, tsr, 1, dev_prev),
        send(tt, tr.at[2], ts, tsr, 2, at(kx, y + 2, flip(core, 1 - ky))),
    ]

    def tcopy(to, slot_core):
        return copy(tt, tr.at[3 + slot_core], ts.at[3 + to], tsr.at[3 + slot_core], at(1 - kx, y, to))

    for c in range(2):
        tcopy(c, core).start()
    sum_a.second()
    cp_rel.wait()
    cp_fr = send(relay, y2buf.at[pre], gs, gr, 7, at(kx, y + 1, flip(core, ((y + 1) % 4) // 2)))
    sum_a.third()
    for c in tcopies:
        c.wait()
    for c in range(2):
        tcopy(c, core).wait_send()
        tcopy(c, c).wait_recv()

    def pair(first, second):
        return 1.0 / jnp.concatenate([first[:, 0:64], second[:, 0:64]], axis=1)

    def fill(col, table):
        up = (TOP / table.T)[0:64]
        for r in range(CYCLES):
            col[r] = jnp.broadcast_to(up[:, r : r + 1], (64, 128))

    mine_t, sib_t, f0_t, f1_t = tt[...], tr[0], tr[3], tr[4]
    row_o[...] = jnp.where(core == 0, pair(mine_t, sib_t), pair(sib_t, mine_t))
    row_f[...] = pair(f0_t, f1_t)
    row_2[...] = pair(mine_t, jnp.where(core == 0, f0_t, f1_t))
    fill(col_y1, tr[1])

    here = kx * 4 + y
    near = kx * 4 + (y + 1) % 4
    prev = kx * 4 + (y + 3) % 4
    opp = kx * 4 + (y + 2) % 4
    cross = (1 - kx) * 4 + y
    cross_near = (1 - kx) * 4 + (y + 1) % 4
    cross_prev = (1 - kx) * 4 + (y + 3) % 4
    cross_opp = (1 - kx) * 4 + (y + 2) % 4

    def place(j, chip, value):
        value = value * (count(j) * (1.0 / TOP))
        out_ref[j, :, pl.ds(pl.multiple_of(chip * 128, 128), 128)] = value

    def ordered(k, local, remote):
        first = jnp.where(k == 0, local, remote)
        second = jnp.where(k == 0, remote, local)
        return jnp.concatenate([first, second], axis=1)

    def count(j):
        return tt[pl.ds(pix * 4 + j, 1), 64:65]

    def final_a():
        for j in range(4):
            lanes = row_o[pl.ds(pix * 4 + j, 1), :]
            up = (TOP / jnp.broadcast_to(tt[pl.ds(pix * 4 + j, 1), :], (8, 128)).T)[0:64, 0:1]
            place(j, here, sum_a.total(j) * up * lanes)

    def final_b():
        for j in range(4):
            b = sum_b.total(j)
            s1[j] = encode(b)
            bt = b.T
            kept0[j] = jnp.where(core == 0, bt[0:64], bt[64:128])
            s7[j] = encode(fold(jnp.where(core == 0, bt[64:128], bt[0:64])))
        return [
            send(s1, r1, fs, fr, 0, near_core),
            send(s7, r7, fs, fr, 1, dev_sib),
        ]

    def copy4(to, landing):
        return copy(s4.at[to], r4.at[landing], fs.at[2 + to], fr.at[2 + landing], at(1 - kx, y, to))

    def final_d():
        for j in range(4):
            g = sum_d.total(j)
            s2[j] = encode(g[0:64])
            dt = g[0:64].T
            s4[0, j] = encode(fold(dt[0:64]))
            s4[1, j] = encode(fold(dt[64:128]))
            s6[j] = encode(g[64:96])
            kept1[j] = unfold(g[64:96]).T
        for c in range(2):
            copy4(c, core).start()
        return [
            send(s2, r2, fs, fr, 4, near_core),
            send(s6, r6, fs, fr, 5, at(1 - kx, y, k1)),
        ]

    def final_c():
        for j in range(4):
            e = sum_c.total(j)
            s3[j] = encode(e)
            et = e.T
            kept2[j] = et[0:64]
            s5[j] = encode(fold(et[64:128]))
        return [
            send(s3, r3, fs, fr, 6, at(kx, y + 2, k2)),
            send(s5, r5, fs, fr, 7, at(1 - kx, y, core)),
        ]

    cp_f.wait()
    fw_f = send(fbuf.at[every, mine], fbuf.at[every, mine], gs, gr, 4, dev_sib)
    cp_y1q.wait()
    cycles(gram_b)
    sum_b.first()
    fill(col_f, jnp.where(k1 == 0, f0_t, f1_t))
    fw_f.wait()
    cycles(gram_d)
    sum_d.first()
    sum_a.last()
    final_a()
    fill(col_y2, tr[2])
    sum_b.second()
    cp_fp.wait()
    cp_fr.wait()
    cycles(gram_c)
    sum_c.first()
    sum_b.third()
    sum_d.second()
    sum_b.last()
    out_b = final_b()
    sum_d.third()
    sum_c.second()
    sum_d.last()
    out_d = final_d()
    sum_c.third()
    for c in out_b:
        c.wait()
    for j in range(4):
        place(j, near, ordered(core, kept0[j], unfold(decode(r7[j]))))
        place(j, prev, decode(r1[j]))
    sum_c.last()
    out_c = final_c()

    for c in range(2):
        copy4(c, core).wait_send()
        copy4(c, c).wait_recv()
    for c in out_d:
        c.wait()
    for j in range(4):
        place(j, cross_near, jnp.concatenate([unfold(decode(r4[0, j])), unfold(decode(r4[1, j]))], axis=1))
        place(j, cross_prev, decode(r2[j]))
        place(j, cross, ordered(k1, kept1[j], unfold(decode(r6[j]))))
    for c in out_c:
        c.wait()
    for j in range(4):
        far = decode(r3[j])
        place(j, opp, ordered(k2, kept2[j], far[:, 0:64]))
        place(j, cross_opp, ordered(k2, unfold(decode(r5[j])), far[:, 64:128]))


def per_device(intensity, labels):
    tile_lab = labels.reshape(-1, 128)[:, 0]
    cycles = jnp.arange(CYCLES, dtype=jnp.int32)
    first = jnp.sum((tile_lab[None, :] < cycles[:, None]).astype(jnp.int32), axis=1)
    count = jnp.sum((tile_lab[None, :] == cycles[:, None]).astype(jnp.int32), axis=1)
    places = jnp.minimum(first, tile_lab.shape[0] - CAP)
    low = (first - places) * 128
    high = low + count * 128
    lane = jnp.arange(CAP * 128, dtype=jnp.int32)[None, :]
    masks = ((lane >= low[:, None]) & (lane < high[:, None])).astype(F32)
    counts = jnp.broadcast_to((count * 128).astype(F32)[:, None], (CYCLES, 128))
    pix_dev = intensity.shape[1]
    dma = pltpu.SemaphoreType.DMA

    def sums(rows, code):
        halves = [
            pltpu.VMEM((2, 2, 2, 2, rows, 128), code),
            pltpu.VMEM((2, 2, 2, rows, 128), code),
            pltpu.VMEM((4, rows, 128), code),
        ]
        return [
            pltpu.VMEM((2, 4, 4, rows, 128), F32),
            *halves,
            *halves,
            dma((7,)),
            dma((7,)),
        ]

    big = pltpu.VMEM((4, 64, 128), CODE)
    small = pltpu.VMEM((4, 32, 128), CODE)
    messages = [big, big, big, pltpu.VMEM((2, 4, 32, 128), CODE), small, small, small]
    kept = pltpu.VMEM((4, 64, 64), F32)
    tiles = pix_dev // 128
    return pl.pallas_call(
        kernel,
        out_shape=jax.ShapeDtypeStruct((4, 64, 1024), F32),
        in_specs=[
            pl.BlockSpec(memory_space=pltpu.SMEM),
            pl.BlockSpec(memory_space=pltpu.VMEM),
            pl.BlockSpec(memory_space=pltpu.VMEM),
            pl.BlockSpec(memory_space=pltpu.HBM),
        ],
        out_specs=pl.BlockSpec(memory_space=pltpu.VMEM),
        scratch_shapes=[
            pltpu.VMEM((FRAMES_DEV, pix_dev), BF16),
            pltpu.VMEM((tiles, FRAMES_DEV, 128), BF16),
            pltpu.VMEM((tiles, 2 * FRAMES_DEV, 128), BF16),
            pltpu.VMEM((tiles, 2 * FRAMES_DEV, 128), BF16),
            pltpu.VMEM((tiles, FRAMES_DEV, 128), BF16),
            pltpu.VMEM((tiles, FRAMES_DEV, 128), BF16),
            pltpu.VMEM((RELAYED, FRAMES_DEV, 128), BF16),
            pltpu.VMEM((CYCLES, 128), F32),
            pltpu.VMEM((7, CYCLES, 128), F32),
            pltpu.VMEM((CYCLES, 128), F32),
            pltpu.VMEM((5, CYCLES, 128), F32),
            *[pltpu.VMEM((CYCLES, FRAMES_DEV, 128), F32)] * 3,
            *[pltpu.VMEM((CYCLES, 128), F32)] * 3,
            *[ref for n, rows in enumerate(SUMS) for ref in sums(rows, CODE if n else F32)],
            *messages,
            *messages,
            kept,
            kept,
            kept,
            dma,
            dma((8,)),
            dma((8,)),
            dma((7,)),
            dma((7,)),
            dma((5,)),
            dma((5,)),
            dma((8,)),
            dma((8,)),
        ],
        compiler_params=pltpu.CompilerParams(
            collective_id=0, has_side_effects=True, vmem_limit_bytes=48 * 2**20
        ),
    )(places, masks, counts, intensity)


def solution(mesh):
    placed = (P("tm", "pix"), P("pix"))
    return jax.shard_map(
        per_device, mesh=mesh, in_specs=placed, out_specs=P("pix", "tm", None), check_vma=False
    )
```

time: 333 us -> 78.4 us (0.24)
  waiting for transfers between devices: 222 us -> 0 us
  Pallas kernels: 0 us -> 74.9 us
  blocking collectives: 56.8 us -> 0 us
  matrix products: 18.3 us -> 0 us
  between operations: 14.2 us -> 0.04 us
  local copies, waits for them, and re-layouts: 14.4 us -> 3.12 us
  other arithmetic: 7.49 us -> 0.2 us
    all_gather x1 -> x0, waiting for transfers between devices: 190 us -> none  [per_device(): raw = pair_block(grouped, lax.all_gather(grouped, 'tm', axis=1, tiled=True))]
    pallas_call x0 -> x1, Pallas kernels: none -> 74.9 us  [per_device(): pl.pallas_call(kernel, out_shape=jax.ShapeDtypeStruct((4, 64, 1024), F32)...]
    reduce_scatter x1 -> x0, waiting for transfers between devices: 31.9 us -> none  [per_device(): lax.psum_scatter(raw, 'pix', scatter_dimension=0, tiled=True)]
    unnamed x1 -> x0, blocking collectives: 30.1 us -> none
    all_gather x1 -> x0, blocking collectives: 26.7 us -> none  [per_device(): every_total = lax.all_gather(own_totals, 'tm', axis=1, tiled=True)]
    dot_general x1 -> x0, matrix products: 18.3 us -> none  [pair_block(): jnp.einsum('rfp,rgp->rfg', left, right, preferred_element_type=jnp.float32)]
    gather x8 -> x0, local copies, waits for them, and re-layouts: 11.1 us -> none  [the longest x3 9.5 us: group_tiles(): picked = jnp.take(padded, index.reshape(-1), axis=1)]
    reduce_sum x2 -> x1, other arithmetic: 3.85 us -> 0.12 us  [per_device(): jnp.sum((tile_lab[None, :] == cycles[:, None]).astype(jnp.int32), axis=1)]
  transfers between devices with their start and end apart: 2 -> 0, of which waited for: 2 -> 0; matrix products, arithmetic and copies ran while one was open for 0% -> 0% of each run, Pallas kernels for 0% -> 0%
where the time goes in v2:
time: 78.4 us; the launch traced here: 78.2 us
  Pallas kernels  74.9 us (96%)
  local copies, waits for them, and re-layouts  3.12 us (4%)
    pallas_call x1, Pallas kernels, per_device(): pl.pallas_call(kernel, out_shape=jax.ShapeDtypeStruct((4, 64, 1024), F32)...  74.9 us
    unnamed x3, local copies, waits for them, and re-layouts  2.19 us

profile of v2, /device:TPU:1, one launch (start us, length us, event | category | flops | bytes accessed | tf_op | source)
XLA Modules:
  0.0 78.2 jit_solution(7230458623185694768)
XLA Ops:
  0.0 0.9 %slice_reduce_fusion = s32[64]{0:T(128)S(1)} fusion(s32[64,128]{1,0:T(8,128)} %bitcast.1), kind=kLoop, calls=%fused_computation.4 | loop fusion | bytes 512 | tf_op jit(solution)/shard_map/slice | solution.py:404
  0.9 0.1 convert_reduce_fusion
  1.0 0.1 broadcast_in_dim.2.counts
  1.1 0.1 fusion.1.masks
  1.2 0.0 copy-start
  1.2 1.2 %copy-done = bf16[64,8192]{1,0:T(8,128)(2,1)S(1)} copy-done((bf16[64,8192]{1,0:T(8,128)(2,1)S(1)}, bf16[64,8192]{1,0:T(8,128)(2,1)}, u32[]{:S(2)}) %copy-start) | copy-done | bytes 1048600
  2.4 74.9 %shard_map.28 = f32[4,64,1024]{2,1,0:T(8,128)S(1)} custom-call(s32[32]{0:T(128)S(1)} %get-tuple-element.10.places, f32[32,512]{1,0:T(8,128)S(1)} %fusion.1.masks, f32[32,128]{1,0:T(8,128)S(1)} %broadcast_in_dim.2.counts, bf16[64,8192]{1,0:T(8,128)(2,1)S(1)} %copy-done), custom_call_target="tpu_custom_call" | custom-call | tf_op jit(solution)/shard_map/pallas_call | solution.py:436
  77.3 1.0 %copy.4 = f32[4,64,1024]{2,1,0:T(8,128)} copy(f32[4,64,1024]{2,1,0:T(8,128)S(1)} %shard_map.28) | data formatting | bytes 2097152
  (1 shorter events, 0.0 us)
Async XLA Ops:
  1.2 1.2 %copy-start = (bf16[64,8192]{1,0:T(8,128)(2,1)S(1)}, bf16[64,8192]{1,0:T(8,128)(2,1)}, u32[]{:S(2)}) copy-start(bf16[64,8192]{1,0:T(8,128)(2,1)} %x_ref.1) | copy-start | bytes 3145732

commit v3 on v2

--- a/solution.py
+++ b/solution.py
@@ -14,7 +14,8 @@
 TOP = 32768.0
 STEPS = 2048.0
 CODE = jnp.int16
-SUMS = (64, 64, 96, 64)
+ROWS_A = 64
+DIRECT = (64, 96, 64)
 RELAYED = 44
 
 
@@ -51,7 +52,8 @@
     part, landed, tt, tr = take(4)
     col_y1, col_y2, col_f = take(3)
     row_o, row_f, row_2 = take(3)
-    sets = [take(9) for _ in SUMS]
+    set_a = take(9)
+    sets = [take(5) for _ in DIRECT]
     s1, s2, s3, s4, s5, s6, s7 = take(7)
     r1, r2, r3, r4, r5, r6, r7 = take(7)
     kept0, kept1, kept2 = take(3)
@@ -113,9 +115,8 @@
     pre = pl.ds(0, RELAYED)
     post = pl.ds(RELAYED, obuf.shape[0] - RELAYED)
     dev_prev = at(kx, y + 3, core)
-    cp_y1p = send(ownb.at[post], y1buf.at[post], gs, gr, 1, dev_prev)
+    cp_y1 = send(ownb, y1buf, gs, gr, 1, dev_prev)
     cp_rel = send(ownb.at[pre], relay, gs, gr, 2, near_core)
-    cp_y1q = send(ownb.at[pre], y1buf.at[pre], gs, gr, 5, dev_prev)
     cp_sib = send(ownb, obuf.at[every, mine], gs, gr, 0, dev_sib)
 
     def span(r):
@@ -134,7 +135,7 @@
         def _(r):
             body(r)
 
-    ga, gb, gd, gc = [q[0] for q in sets]
+    ga = set_a[0]
     whole = slice(None)
 
     def scaled(r, g, col, rows):
@@ -153,7 +154,7 @@
     def gram_b(r):
         tile, mask = span(r)
         right = window(obuf, tile, whole) * mask[0:1]
-        gb[slot(r)] = scaled(r, nt(window(y1buf, tile, whole), right), col_y1[r], row_o)
+        return scaled(r, nt(window(y1buf, tile, whole), right), col_y1[r], row_o)
 
     def two(tile, mask):
         right = jnp.concatenate([window(obuf, tile, mine), window(fbuf, tile, mine)], axis=0)
@@ -161,73 +162,99 @@
 
     def gram_d(r):
         tile, mask = span(r)
-        i, k, j = slot(r)
         right = window(fbuf, tile, whole) * mask[0:1]
-        gd[i, k, j, 0:64] = scaled(r, nt(window(y1buf, tile, whole), right), col_y1[r], row_f)
+        first = scaled(r, nt(window(y1buf, tile, whole), right), col_y1[r], row_f)
         fk = pl.ds(k1 * 64, 64)
         right = window(obuf, tile, mine) * mask[0:1]
         g = nt(window(fbuf, tile, fk), right)
         g = g * col_f[r, :, 0:64] * row_2[pl.ds(r, 1), 0:64]
-        gd[i, k, j, 64:96] = fold(g)
+        return jnp.concatenate([first, fold(g)], axis=0)
 
     def gram_c(r):
         tile, mask = span(r)
         g = nt(window(y2buf, tile, whole), two(tile, mask))
-        gc[slot(r)] = scaled(r, g, col_y2[r], row_2)
+        return scaled(r, g, col_y2[r], row_2)
 
     lo, hi = pl.ds(0, 2), pl.ds(2, 2)
     both_x = pl.ds(0, 2)
 
     class Sum:
-        def __init__(self, coded, g, e1, e2, e3, r1, r2, r3, ss, rs):
-            self.encode = encode if coded else (lambda v: v)
-            self.decode = decode if coded else (lambda v: v)
+        def __init__(self, g, e1, e2, e3, r1, r2, r3, ss, rs):
             self.g, self.e, self.r = g, (e1, e2, e3), (r1, r2, r3)
             self.ss, self.rs = ss, rs
 
         def first(self):
-            g, e1, r1 = self.g, self.e[0], self.r[0]
-            self.c1 = []
-            for w, (za, zb) in enumerate(((z2, z2), (z1, z3))):
-                for p, (js, zz, d) in enumerate(((0, za, dev_z1), (2, zb, dev_z3))):
-                    for i in range(2):
-                        for j in range(2):
-                            e1[p, w, i, j] = self.encode(g[i, zz, js + j])
-                    self.c1.append(send(e1.at[p, w], r1.at[p, w], self.ss, self.rs, 2 * w + p, d))
+            g, r1 = self.g, self.r[0]
+            self.c1 = [
+                send(g.at[both_x, z2, lo], r1.at[0, 0], self.ss, self.rs, 0, dev_z1),
+                send(g.at[both_x, z2, hi], r1.at[1, 0], self.ss, self.rs, 1, dev_z3),
+                send(g.at[both_x, z1, lo], r1.at[0, 1], self.ss, self.rs, 2, dev_z1),
+                send(g.at[both_x, z3, hi], r1.at[1, 1], self.ss, self.rs, 3, dev_z3),
+            ]
 
         def second(self):
-            g, e2, r1, r2 = self.g, self.e[1], self.r[0], self.r[1]
+            g, r1, r2 = self.g, self.r[0], self.r[1]
             self.c2 = []
             for p, (js, zz, d) in enumerate(((0, z3, dev_z3), (2, z1, dev_z1))):
                 self.c1[p].wait()
                 for i in range(2):
                     for j in range(2):
-                        e2[p, i, j] = self.encode(g[i, zz, js + j] + self.decode(r1[p, 0, i, j]))
-                self.c2.append(send(e2.at[p], r2.at[p], self.ss, self.rs, 4 + p, d))
+                        g[i, zz, js + j] += r1[p, 0, i, j]
+                self.c2.append(send(g.at[both_x, zz, pl.ds(js, 2)], r2.at[p], self.ss, self.rs, 4 + p, d))
             for p in range(2):
                 self.c1[2 + p].wait()
                 for i in range(2):
                     for j in range(2):
-                        g[i, z, 2 * p + j] += self.decode(r1[p, 1, i, j])
+                        g[i, z, 2 * p + j] += r1[p, 1, i, j]
 
         def third(self):
-            g, e3, r2 = self.g, self.e[2], self.r[1]
+            g, r2 = self.g, self.r[1]
             for p in range(2):
                 self.c2[p].wait()
                 for j in range(2):
-                    e3[2 * p + j] = self.encode(g[1 - xl, z, 2 * p + j] + self.decode(r2[p, 1 - xl, j]))
-            self.c3 = send(e3, self.r[2], self.ss, self.rs, 6, dev_x)
+                    g[1 - xl, z, 2 * p + j] += r2[p, 1 - xl, j]
+            self.c3 = send(g.at[1 - xl, z], self.r[2], self.ss, self.rs, 6, dev_x)
             for p in range(2):
                 for j in range(2):
-                    g[xl, z, 2 * p + j] += self.decode(r2[p, xl, j])
+                    g[xl, z, 2 * p + j] += r2[p, xl, j]
 
         def last(self):
             self.c3.wait()
 
         def total(self, j):
-            return self.g[xl, z, j] + self.decode(self.r[2][j])
-
-    sum_a, sum_b, sum_d, sum_c = [Sum(n > 0, *q) for n, q in enumerate(sets)]
+            return self.g[xl, z, j] + self.r[2][j]
+
+    class Direct:
+        def __init__(self, body, own, e, r, ss, rs):
+            self.body, self.own, self.e, self.r, self.ss, self.rs = body, own, e, r, ss, rs
+
+        def copy(self, q):
+            k = q - 1
+            return copy(self.e.at[k], self.r.at[k], self.ss.at[k], self.rs.at[k], (tm, (pix + q) % 8))
+
+        def run(self):
+            @pl.loop(1, 8)
+            def _(q):
+                p = (pix + q) % 8
+                for j in range(4):
+                    self.e[q - 1, j] = encode(self.body(p * 4 + j))
+                self.copy(q).start()
+
+            for j in range(4):
+                self.own[j] = self.body(pix * 4 + j)
+
+        def wait(self):
+            for q in range(1, 8):
+                self.copy(q).wait()
+
+        def total(self, j):
+            value = self.own[j]
+            for q in range(7):
+                value = value + decode(self.r[q, j])
+            return value
+
+    sum_a = Sum(*set_a)
+    sum_b, sum_d, sum_c = [Direct(body, *q) for body, q in zip((gram_b, gram_d, gram_c), sets)]
 
     cycles(totals_own)
     cp = []
@@ -237,8 +264,6 @@
     cp_sib.wait()
     cycles(gram_a)
     sum_a.first()
-    cp_y1p.wait()
-    cp_fp = send(y1buf.at[post], y2buf.at[post], gs, gr, 6, at(kx, y + 3, flip(core, ((y + 3) % 4) // 2)))
     total = part[...]
     for q in range(7):
         cp[q].wait()
@@ -259,6 +284,8 @@
     cp_rel.wait()
     cp_fr = send(relay, y2buf.at[pre], gs, gr, 7, at(kx, y + 1, flip(core, ((y + 1) % 4) // 2)))
     sum_a.third()
+    cp_y1.wait()
+    cp_fp = send(y1buf.at[post], y2buf.at[post], gs, gr, 6, at(kx, y + 3, flip(core, ((y + 3) % 4) // 2)))
     for c in tcopies:
         c.wait()
     for c in range(2):
@@ -351,37 +378,27 @@
 
     cp_f.wait()
     fw_f = send(fbuf.at[every, mine], fbuf.at[every, mine], gs, gr, 4, dev_sib)
-    cp_y1q.wait()
-    cycles(gram_b)
-    sum_b.first()
+    sum_b.run()
     fill(col_f, jnp.where(k1 == 0, f0_t, f1_t))
     fw_f.wait()
-    cycles(gram_d)
-    sum_d.first()
+    sum_d.run()
+    fill(col_y2, tr[2])
+    cp_fp.wait()
+    cp_fr.wait()
+    sum_c.run()
     sum_a.last()
     final_a()
-    fill(col_y2, tr[2])
-    sum_b.second()
-    cp_fp.wait()
-    cp_fr.wait()
-    cycles(gram_c)
-    sum_c.first()
-    sum_b.third()
-    sum_d.second()
-    sum_b.last()
+    sum_b.wait()
     out_b = final_b()
-    sum_d.third()
-    sum_c.second()
-    sum_d.last()
+    sum_d.wait()
     out_d = final_d()
-    sum_c.third()
+    sum_c.wait()
+    out_c = final_c()
     for c in out_b:
         c.wait()
     for j in range(4):
         place(j, near, ordered(core, kept0[j], unfold(decode(r7[j]))))
         place(j, prev, decode(r1[j]))
-    sum_c.last()
-    out_c = final_c()
 
     for c in range(2):
         copy4(c, core).wait_send()
@@ -414,19 +431,15 @@
     pix_dev = intensity.shape[1]
     dma = pltpu.SemaphoreType.DMA
 
-    def sums(rows, code):
-        halves = [
-            pltpu.VMEM((2, 2, 2, 2, rows, 128), code),
-            pltpu.VMEM((2, 2, 2, rows, 128), code),
-            pltpu.VMEM((4, rows, 128), code),
-        ]
-        return [
-            pltpu.VMEM((2, 4, 4, rows, 128), F32),
-            *halves,
-            *halves,
-            dma((7,)),
-            dma((7,)),
-        ]
+    halves = [
+        pltpu.VMEM((2, 2, 2, 2, ROWS_A, 128), F32),
+        pltpu.VMEM((2, 2, 2, ROWS_A, 128), F32),
+        pltpu.VMEM((4, ROWS_A, 128), F32),
+    ]
+
+    def direct(rows):
+        slabs = pltpu.VMEM((7, 4, rows, 128), CODE)
+        return [pltpu.VMEM((4, rows, 128), F32), slabs, slabs, dma((7,)), dma((7,))]
 
     big = pltpu.VMEM((4, 64, 128), CODE)
     small = pltpu.VMEM((4, 32, 128), CODE)
@@ -457,7 +470,12 @@
             pltpu.VMEM((5, CYCLES, 128), F32),
             *[pltpu.VMEM((CYCLES, FRAMES_DEV, 128), F32)] * 3,
             *[pltpu.VMEM((CYCLES, 128), F32)] * 3,
-            *[ref for n, rows in enumerate(SUMS) for ref in sums(rows, CODE if n else F32)],
+            pltpu.VMEM((2, 4, 4, ROWS_A, 128), F32),
+            *halves,
+            *halves,
+            dma((7,)),
+            dma((7,)),
+            *[ref for rows in DIRECT for ref in direct(rows)],
             *messages,
             *messages,
             kept,

time: 78.4 us -> 70.3 us (0.90)
  Pallas kernels: 74.9 us -> 66.7 us
    pallas_call x1, Pallas kernels: 74.9 us -> 66.7 us  [per_device(): pl.pallas_call(kernel, out_shape=jax.ShapeDtypeStruct((4, 64, 1024), F32)...]
where the time goes in v3:
time: 70.3 us; the launch traced here: 70.1 us
  Pallas kernels  66.7 us (95%)
  local copies, waits for them, and re-layouts  3.12 us (4%)
    pallas_call x1, Pallas kernels, per_device(): pl.pallas_call(kernel, out_shape=jax.ShapeDtypeStruct((4, 64, 1024), F32)...  66.7 us
    unnamed x3, local copies, waits for them, and re-layouts  2.19 us

profile of v3, /device:TPU:1, one launch (start us, length us, event | category | flops | bytes accessed | tf_op | source)
XLA Modules:
  0.0 70.1 jit_solution(470625749477281307)
XLA Ops:
  0.0 0.9 %slice_reduce_fusion = s32[64]{0:T(128)S(1)} fusion(s32[64,128]{1,0:T(8,128)} %bitcast.1), kind=kLoop, calls=%fused_computation.4 | loop fusion | bytes 512 | tf_op jit(solution)/shard_map/slice | solution.py:421
  0.9 0.1 convert_reduce_fusion
  1.0 0.1 broadcast_in_dim.2.counts
  1.1 0.1 fusion.1.masks
  1.2 0.0 copy-start
  1.2 1.2 %copy-done = bf16[64,8192]{1,0:T(8,128)(2,1)S(1)} copy-done((bf16[64,8192]{1,0:T(8,128)(2,1)S(1)}, bf16[64,8192]{1,0:T(8,128)(2,1)}, u32[]{:S(2)}) %copy-start) | copy-done | bytes 1048600
  2.4 66.7 %shard_map.28 = f32[4,64,1024]{2,1,0:T(8,128)S(1)} custom-call(s32[32]{0:T(128)S(1)} %get-tuple-element.10.places, f32[32,512]{1,0:T(8,128)S(1)} %fusion.1.masks, f32[32,128]{1,0:T(8,128)S(1)} %broadcast_in_dim.2.counts, bf16[64,8192]{1,0:T(8,128)(2,1)S(1)} %copy-done), custom_call_target="tpu_custom_call" | custom-call | tf_op jit(solution)/shard_map/pallas_call | solution.py:449
  69.1 1.0 %copy.4 = f32[4,64,1024]{2,1,0:T(8,128)} copy(f32[4,64,1024]{2,1,0:T(8,128)S(1)} %shard_map.28) | data formatting | bytes 2097152
  (1 shorter events, 0.0 us)
Async XLA Ops:
  1.2 1.2 %copy-start = (bf16[64,8192]{1,0:T(8,128)(2,1)S(1)}, bf16[64,8192]{1,0:T(8,128)(2,1)}, u32[]{:S(2)}) copy-start(bf16[64,8192]{1,0:T(8,128)(2,1)} %x_ref.1) | copy-start | bytes 3145732

commit v4 on v3

--- a/solution.py
+++ b/solution.py
@@ -99,7 +99,6 @@
         block = xv[:, t * 128 : t * 128 + 128]
         ownb[t] = block
         obuf[t, mine] = block
-    pl.semaphore_wait(barrier, len(friends))
 
     def copy(src, dst, ss, rs, d):
         return pltpu.make_async_remote_copy(
@@ -112,13 +111,6 @@
         return r
 
     every = pl.ds(0, obuf.shape[0])
-    pre = pl.ds(0, RELAYED)
-    post = pl.ds(RELAYED, obuf.shape[0] - RELAYED)
-    dev_prev = at(kx, y + 3, core)
-    cp_y1 = send(ownb, y1buf, gs, gr, 1, dev_prev)
-    cp_rel = send(ownb.at[pre], relay, gs, gr, 2, near_core)
-    cp_sib = send(ownb, obuf.at[every, mine], gs, gr, 0, dev_sib)
-
     def span(r):
         tile = places[r]
         mask = jnp.broadcast_to(masks[pl.ds(r, 1), :], (8, CAP * 128)).astype(BF16)
@@ -257,10 +249,17 @@
     sum_b, sum_d, sum_c = [Direct(body, *q) for body, q in zip((gram_b, gram_d, gram_c), sets)]
 
     cycles(totals_own)
+    pl.semaphore_wait(barrier, len(friends))
     cp = []
     for q in range(1, 8):
         cp.append(send(part, landed.at[q - 1], ps, pr, q - 1, (tm, (pix + q) % 8)))
+    pre = pl.ds(0, RELAYED)
+    post = pl.ds(RELAYED, obuf.shape[0] - RELAYED)
+    dev_prev = at(kx, y + 3, core)
     cp_f = send(ownb, fbuf.at[every, mine], gs, gr, 3, at(1 - kx, y, core))
+    cp_y1 = send(ownb, y1buf, gs, gr, 1, dev_prev)
+    cp_rel = send(ownb.at[pre], relay, gs, gr, 2, near_core)
+    cp_sib = send(ownb, obuf.at[every, mine], gs, gr, 0, dev_sib)
     cp_sib.wait()
     cycles(gram_a)
     sum_a.first()

time: 70.3 us -> 68.8 us (0.979)
  Pallas kernels: 66.7 us -> 65.2 us
    pallas_call x1, Pallas kernels: 66.7 us -> 65.2 us  [per_device(): pl.pallas_call(kernel, out_shape=jax.ShapeDtypeStruct((4, 64, 1024), F32)...]
where the time goes in v4:
time: 68.8 us; the launch traced here: 68.6 us
  Pallas kernels  65.2 us (95%)
  local copies, waits for them, and re-layouts  3.12 us (5%)
    pallas_call x1, Pallas kernels, per_device(): pl.pallas_call(kernel, out_shape=jax.ShapeDtypeStruct((4, 64, 1024), F32)...  65.2 us
    unnamed x3, local copies, waits for them, and re-layouts  2.19 us

profile of v4, /device:TPU:1, one launch (start us, length us, event | category | flops | bytes accessed | tf_op | source)
XLA Modules:
  0.0 68.6 jit_solution(7897536490471818410)
XLA Ops:
  0.0 0.9 %slice_reduce_fusion = s32[64]{0:T(128)S(1)} fusion(s32[64,128]{1,0:T(8,128)} %bitcast.1), kind=kLoop, calls=%fused_computation.4 | loop fusion | bytes 512 | tf_op jit(solution)/shard_map/slice | solution.py:420
  0.9 0.1 convert_reduce_fusion
  1.0 0.1 broadcast_in_dim.2.counts
  1.1 0.1 fusion.1.masks
  1.2 0.0 copy-start
  1.2 1.2 %copy-done = bf16[64,8192]{1,0:T(8,128)(2,1)S(1)} copy-done((bf16[64,8192]{1,0:T(8,128)(2,1)S(1)}, bf16[64,8192]{1,0:T(8,128)(2,1)}, u32[]{:S(2)}) %copy-start) | copy-done | bytes 1048600
  2.4 65.2 %shard_map.28 = f32[4,64,1024]{2,1,0:T(8,128)S(1)} custom-call(s32[32]{0:T(128)S(1)} %get-tuple-element.10.places, f32[32,512]{1,0:T(8,128)S(1)} %fusion.1.masks, f32[32,128]{1,0:T(8,128)S(1)} %broadcast_in_dim.2.counts, bf16[64,8192]{1,0:T(8,128)(2,1)S(1)} %copy-done), custom_call_target="tpu_custom_call" | custom-call | tf_op jit(solution)/shard_map/pallas_call | solution.py:448
  67.6 1.0 %copy.4 = f32[4,64,1024]{2,1,0:T(8,128)} copy(f32[4,64,1024]{2,1,0:T(8,128)S(1)} %shard_map.28) | data formatting | bytes 2097152
  (1 shorter events, 0.0 us)
Async XLA Ops:
  1.2 1.2 %copy-start = (bf16[64,8192]{1,0:T(8,128)(2,1)S(1)}, bf16[64,8192]{1,0:T(8,128)(2,1)}, u32[]{:S(2)}) copy-start(bf16[64,8192]{1,0:T(8,128)(2,1)} %x_ref.1) | copy-start | bytes 3145732

commit v5 on v4

--- a/solution.py
+++ b/solution.py
@@ -15,7 +15,8 @@
 STEPS = 2048.0
 CODE = jnp.int16
 ROWS_A = 64
-DIRECT = (64, 96, 64)
+MIXED = (64, 96)
+DIRECT = 64
 RELAYED = 44
 
 
@@ -53,7 +54,8 @@
     col_y1, col_y2, col_f = take(3)
     row_o, row_f, row_2 = take(3)
     set_a = take(9)
-    sets = [take(5) for _ in DIRECT]
+    mixed = [take(12) for _ in MIXED]
+    set_c = take(5)
     s1, s2, s3, s4, s5, s6, s7 = take(7)
     r1, r2, r3, r4, r5, r6, r7 = take(7)
     kept0, kept1, kept2 = take(3)
@@ -246,7 +248,90 @@
             return value
 
     sum_a = Sum(*set_a)
-    sum_b, sum_d, sum_c = [Direct(body, *q) for body, q in zip((gram_b, gram_d, gram_c), sets)]
+    class Mixed:
+        def __init__(self, body, keepx, keepz, ex, ez, e2x, e2z, rx, rz, r2x, r2z, ss, rs):
+            self.body, self.keepx, self.keepz = body, keepx, keepz
+            self.ex, self.ez, self.e2x, self.e2z = ex, ez, e2x, e2z
+            self.rx, self.rz, self.r2x, self.r2z = rx, rz, r2x, r2z
+            self.ss, self.rs = ss, rs
+
+        def go(self, src, dst, k, d):
+            return copy(src, dst, self.ss.at[k], self.rs.at[k], d)
+
+        def x_first(self, k):
+            return self.go(self.ex.at[k], self.rx.at[k], k, dev_x)
+
+        def z_first(self, q):
+            d = (tm, xl * 4 + (z + q) % 4)
+            return self.go(self.ez.at[q - 1], self.rz.at[q - 1], 3 + q, d)
+
+        def z_second(self, q):
+            d = (tm, xl * 4 + (z + q) % 4)
+            return self.go(self.e2x.at[q - 1], self.r2x.at[q - 1], 6 + q, d)
+
+        def x_second(self):
+            return self.go(self.e2z, self.r2z, 10, dev_x)
+
+        def run(self):
+            @pl.loop(0, 4)
+            def _(k):
+                for j in range(2):
+                    self.ex[k, j] = encode(self.body(((1 - xl) * 4 + k) * 4 + j))
+                self.x_first(k).start()
+
+            @pl.loop(1, 4)
+            def _(q):
+                for i in range(2):
+                    for j in range(2):
+                        value = self.body((i * 4 + (z + q) % 4) * 4 + 2 + j)
+                        self.ez[q - 1, i, j] = encode(value)
+                self.z_first(q).start()
+
+            @pl.loop(0, 4)
+            def _(k):
+                for j in range(2):
+                    self.keepx[k, j] = self.body((xl * 4 + k) * 4 + j)
+
+            @pl.loop(0, 2)
+            def _(i):
+                for j in range(2):
+                    self.keepz[i, j] = self.body((i * 4 + z) * 4 + 2 + j)
+
+        def mid(self):
+            for k in range(4):
+                self.x_first(k).wait()
+            for q in range(1, 4):
+                k = (z + q) % 4
+                for j in range(2):
+                    self.e2x[q - 1, j] = encode(self.keepx[k, j] + decode(self.rx[k, j]))
+                self.z_second(q).start()
+            for q in range(1, 4):
+                self.z_first(q).wait()
+            for j in range(2):
+                self.e2z[j] = encode(self.over_z(1 - xl, j))
+            self.x_second().start()
+
+        def over_z(self, i, j):
+            value = self.keepz[i, j]
+            for q in range(3):
+                value = value + decode(self.rz[q, i, j])
+            return value
+
+        def wait(self):
+            for q in range(1, 4):
+                self.z_second(q).wait()
+            self.x_second().wait()
+
+        def total(self, j):
+            if j < 2:
+                value = self.keepx[z, j] + decode(self.rx[z, j])
+                for q in range(3):
+                    value = value + decode(self.r2x[q, j])
+                return value
+            return self.over_z(xl, j - 2) + decode(self.r2z[j - 2])
+
+    sum_b, sum_d = Mixed(gram_b, *mixed[0]), Mixed(gram_d, *mixed[1])
+    sum_c = Direct(gram_c, *set_c)
 
     cycles(totals_own)
     pl.semaphore_wait(barrier, len(friends))
@@ -282,7 +367,6 @@
     sum_a.second()
     cp_rel.wait()
     cp_fr = send(relay, y2buf.at[pre], gs, gr, 7, at(kx, y + 1, flip(core, ((y + 1) % 4) // 2)))
-    sum_a.third()
     cp_y1.wait()
     cp_fp = send(y1buf.at[post], y2buf.at[post], gs, gr, 6, at(kx, y + 3, flip(core, ((y + 3) % 4) // 2)))
     for c in tcopies:
@@ -381,10 +465,13 @@
     fill(col_f, jnp.where(k1 == 0, f0_t, f1_t))
     fw_f.wait()
     sum_d.run()
+    sum_a.third()
+    sum_b.mid()
     fill(col_y2, tr[2])
     cp_fp.wait()
     cp_fr.wait()
     sum_c.run()
+    sum_d.mid()
     sum_a.last()
     final_a()
     sum_b.wait()
@@ -435,6 +522,14 @@
         pltpu.VMEM((2, 2, 2, ROWS_A, 128), F32),
         pltpu.VMEM((4, ROWS_A, 128), F32),
     ]
+
+    def two_ways(rows):
+        def codes(*lead):
+            return pltpu.VMEM((*lead, rows, 128), CODE)
+
+        moved = [codes(4, 2), codes(3, 2, 2), codes(3, 2), codes(2)]
+        kept = [pltpu.VMEM((4, 2, rows, 128), F32), pltpu.VMEM((2, 2, rows, 128), F32)]
+        return [*kept, *moved, *moved, dma((11,)), dma((11,))]
 
     def direct(rows):
         slabs = pltpu.VMEM((7, 4, rows, 128), CODE)
@@ -474,7 +569,8 @@
             *halves,
             dma((7,)),
             dma((7,)),
-            *[ref for rows in DIRECT for ref in direct(rows)],
+            *[ref for rows in MIXED for ref in two_ways(rows)],
+            *direct(DIRECT),
             *messages,
             *messages,
             kept,

time: 68.8 us -> 67.9 us (0.987)
  Pallas kernels: 65.2 us -> 64.3 us
    pallas_call x1, Pallas kernels: 65.2 us -> 64.3 us  [per_device(): pl.pallas_call(kernel, out_shape=jax.ShapeDtypeStruct((4, 64, 1024), F32)...]
where the time goes in v5:
time: 67.9 us; the launch traced here: 67.7 us
  Pallas kernels  64.3 us (95%)
  local copies, waits for them, and re-layouts  3.12 us (5%)
    pallas_call x1, Pallas kernels, per_device(): pl.pallas_call(kernel, out_shape=jax.ShapeDtypeStruct((4, 64, 1024), F32)...  64.3 us
    unnamed x3, local copies, waits for them, and re-layouts  2.19 us

profile of v5, /device:TPU:1, one launch (start us, length us, event | category | flops | bytes accessed | tf_op | source)
XLA Modules:
  0.0 67.7 jit_solution(1117268938905491241)
XLA Ops:
  0.0 0.9 %slice_reduce_fusion = s32[64]{0:T(128)S(1)} fusion(s32[64,128]{1,0:T(8,128)} %bitcast.1), kind=kLoop, calls=%fused_computation.4 | loop fusion | bytes 512 | tf_op jit(solution)/shard_map/slice | solution.py:507
  0.9 0.1 convert_reduce_fusion
  1.0 0.1 broadcast_in_dim.2.counts
  1.1 0.1 fusion.1.masks
  1.2 0.0 copy-start
  1.2 1.2 %copy-done = bf16[64,8192]{1,0:T(8,128)(2,1)S(1)} copy-done((bf16[64,8192]{1,0:T(8,128)(2,1)S(1)}, bf16[64,8192]{1,0:T(8,128)(2,1)}, u32[]{:S(2)}) %copy-start) | copy-done | bytes 1048600
  2.4 64.3 %shard_map.28 = f32[4,64,1024]{2,1,0:T(8,128)S(1)} custom-call(s32[32]{0:T(128)S(1)} %get-tuple-element.10.places, f32[32,512]{1,0:T(8,128)S(1)} %fusion.1.masks, f32[32,128]{1,0:T(8,128)S(1)} %broadcast_in_dim.2.counts, bf16[64,8192]{1,0:T(8,128)(2,1)S(1)} %copy-done), custom_call_target="tpu_custom_call" | custom-call | tf_op jit(solution)/shard_map/pallas_call | solution.py:543
  66.7 1.0 %copy.4 = f32[4,64,1024]{2,1,0:T(8,128)} copy(f32[4,64,1024]{2,1,0:T(8,128)S(1)} %shard_map.28) | data formatting | bytes 2097152
  (1 shorter events, 0.0 us)
Async XLA Ops:
  1.2 1.2 %copy-start = (bf16[64,8192]{1,0:T(8,128)(2,1)S(1)}, bf16[64,8192]{1,0:T(8,128)(2,1)}, u32[]{:S(2)}) copy-start(bf16[64,8192]{1,0:T(8,128)(2,1)} %x_ref.1) | copy-start | bytes 3145732

commit v6 on v5

--- a/solution.py
+++ b/solution.py
@@ -273,12 +273,6 @@
             return self.go(self.e2z, self.r2z, 10, dev_x)
 
         def run(self):
-            @pl.loop(0, 4)
-            def _(k):
-                for j in range(2):
-                    self.ex[k, j] = encode(self.body(((1 - xl) * 4 + k) * 4 + j))
-                self.x_first(k).start()
-
             @pl.loop(1, 4)
             def _(q):
                 for i in range(2):
@@ -286,6 +280,12 @@
                         value = self.body((i * 4 + (z + q) % 4) * 4 + 2 + j)
                         self.ez[q - 1, i, j] = encode(value)
                 self.z_first(q).start()
+
+            @pl.loop(0, 4)
+            def _(k):
+                for j in range(2):
+                    self.ex[k, j] = encode(self.body(((1 - xl) * 4 + k) * 4 + j))
+                self.x_first(k).start()
 
             @pl.loop(0, 4)
             def _(k):

time: 67.9 us -> 67.5 us (level)
  no operation moved by 1% of the time
where the time goes in v6:
time: 67.5 us; the launch traced here: 67.3 us
  Pallas kernels  64 us (95%)
  local copies, waits for them, and re-layouts  3.12 us (5%)
    pallas_call x1, Pallas kernels, per_device(): pl.pallas_call(kernel, out_shape=jax.ShapeDtypeStruct((4, 64, 1024), F32)...  64 us
    unnamed x3, local copies, waits for them, and re-layouts  2.19 us

profile of v6, /device:TPU:1, one launch (start us, length us, event | category | flops | bytes accessed | tf_op | source)
XLA Modules:
  0.0 67.3 jit_solution(10956774887172848271)
XLA Ops:
  0.0 0.9 %slice_reduce_fusion = s32[64]{0:T(128)S(1)} fusion(s32[64,128]{1,0:T(8,128)} %bitcast.1), kind=kLoop, calls=%fused_computation.4 | loop fusion | bytes 512 | tf_op jit(solution)/shard_map/slice | solution.py:507
  0.9 0.1 convert_reduce_fusion
  1.0 0.1 broadcast_in_dim.2.counts
  1.1 0.1 fusion.1.masks
  1.2 0.0 copy-start
  1.2 1.2 %copy-done = bf16[64,8192]{1,0:T(8,128)(2,1)S(1)} copy-done((bf16[64,8192]{1,0:T(8,128)(2,1)S(1)}, bf16[64,8192]{1,0:T(8,128)(2,1)}, u32[]{:S(2)}) %copy-start) | copy-done | bytes 1048600
  2.4 64.0 %shard_map.28 = f32[4,64,1024]{2,1,0:T(8,128)S(1)} custom-call(s32[32]{0:T(128)S(1)} %get-tuple-element.10.places, f32[32,512]{1,0:T(8,128)S(1)} %fusion.1.masks, f32[32,128]{1,0:T(8,128)S(1)} %broadcast_in_dim.2.counts, bf16[64,8192]{1,0:T(8,128)(2,1)S(1)} %copy-done), custom_call_target="tpu_custom_call" | custom-call | tf_op jit(solution)/shard_map/pallas_call | solution.py:543
  66.4 1.0 %copy.4 = f32[4,64,1024]{2,1,0:T(8,128)} copy(f32[4,64,1024]{2,1,0:T(8,128)S(1)} %shard_map.28) | data formatting | bytes 2097152
  (1 shorter events, 0.0 us)
Async XLA Ops:
  1.2 1.2 %copy-start = (bf16[64,8192]{1,0:T(8,128)(2,1)S(1)}, bf16[64,8192]{1,0:T(8,128)(2,1)}, u32[]{:S(2)}) copy-start(bf16[64,8192]{1,0:T(8,128)(2,1)} %x_ref.1) | copy-start | bytes 3145732

commit v7 on v6

--- a/solution.py
+++ b/solution.py
@@ -17,7 +17,7 @@
 ROWS_A = 64
 MIXED = (64, 96)
 DIRECT = 64
-RELAYED = 44
+RELAYED = 36
 
 
 def nt(left, right):

time: 67.5 us -> 67.5 us (level)
  no operation moved by 1% of the time
where the time goes in v7:
time: 67.5 us; the launch traced here: 67.3 us
  Pallas kernels  64 us (95%)
  local copies, waits for them, and re-layouts  3.12 us (5%)
    pallas_call x1, Pallas kernels, per_device(): pl.pallas_call(kernel, out_shape=jax.ShapeDtypeStruct((4, 64, 1024), F32)...  64 us
    unnamed x3, local copies, waits for them, and re-layouts  2.19 us

profile of v7, /device:TPU:1, one launch (start us, length us, event | category | flops | bytes accessed | tf_op | source)
XLA Modules:
  0.0 67.3 jit_solution(1076167366734814797)
XLA Ops:
  0.0 0.9 %slice_reduce_fusion = s32[64]{0:T(128)S(1)} fusion(s32[64,128]{1,0:T(8,128)} %bitcast.1), kind=kLoop, calls=%fused_computation.4 | loop fusion | bytes 512 | tf_op jit(solution)/shard_map/slice | solution.py:507
  0.9 0.1 convert_reduce_fusion
  1.0 0.1 broadcast_in_dim.2.counts
  1.1 0.1 fusion.1.masks
  1.2 0.0 copy-start
  1.2 1.2 %copy-done = bf16[64,8192]{1,0:T(8,128)(2,1)S(1)} copy-done((bf16[64,8192]{1,0:T(8,128)(2,1)S(1)}, bf16[64,8192]{1,0:T(8,128)(2,1)}, u32[]{:S(2)}) %copy-start) | copy-done | bytes 1048600
  2.4 64.0 %shard_map.28 = f32[4,64,1024]{2,1,0:T(8,128)S(1)} custom-call(s32[32]{0:T(128)S(1)} %get-tuple-element.10.places, f32[32,512]{1,0:T(8,128)S(1)} %fusion.1.masks, f32[32,128]{1,0:T(8,128)S(1)} %broadcast_in_dim.2.counts, bf16[64,8192]{1,0:T(8,128)(2,1)S(1)} %copy-done), custom_call_target="tpu_custom_call" | custom-call | tf_op jit(solution)/shard_map/pallas_call | solution.py:543
  66.4 1.0 %copy.4 = f32[4,64,1024]{2,1,0:T(8,128)} copy(f32[4,64,1024]{2,1,0:T(8,128)S(1)} %shard_map.28) | data formatting | bytes 2097152
  (1 shorter events, 0.0 us)
Async XLA Ops:
  1.2 1.2 %copy-start = (bf16[64,8192]{1,0:T(8,128)(2,1)S(1)}, bf16[64,8192]{1,0:T(8,128)(2,1)}, u32[]{:S(2)}) copy-start(bf16[64,8192]{1,0:T(8,128)(2,1)} %x_ref.1) | copy-start | bytes 3145732
